TPU v7x, 256 devices: a whole 4x4x8 slice. The times are simulated.
256 devices in a mesh: tok: 32 (over y, z), exp: 8 (over x, core).
Axes of the slice: x: 4, y: 4, z: 8, core: 2. Of those that a mesh axis runs over, the one named last changes fastest.
Arguments:
- tokens: bfloat16 [4096, 5120], P('tok', 'exp'), may hold values from -6 to 6
- cotangent: bfloat16 [4096, 5120], P('tok', 'exp'), may hold values from -1.796875 to 1.796875
- routes: int32 [4096, 6], P('tok'), may hold values from 0 to 31, as said below
- gate_values: float32 [4096, 6], P('tok'), may hold values from 0.1 to 1
- w_gate: bfloat16 [32, 5120, 1024], P('tok', 'exp'), may hold values from -0.078125 to 0.078125
- w_up: bfloat16 [32, 5120, 1024], P('tok', 'exp'), may hold values from -0.078125 to 0.078125
- w_down: bfloat16 [32, 1024, 5120], P('tok', None, 'exp'), may hold values from -0.1875 to 0.1875
Outputs:
- token_grad: bfloat16 [4096, 5120], P('tok', 'exp')
- gate_grad: bfloat16 [32, 5120, 1024], P('tok', 'exp')
- up_grad: bfloat16 [32, 5120, 1024], P('tok', 'exp')
- down_grad: bfloat16 [32, 1024, 5120], P('tok', None, 'exp')
Inputs may be any that keep to these rules, and one draw needn't show every extreme that they name: `routes`: each row names 6 different experts, all within at most 3 of the 8 groups of 4 consecutive expert numbers. Among the 128 rows of one index of tok no expert is named by more than 40 rows, and in every such block some expert is named by exactly 40 rows.
All inputs are finite; a program needn't handle non-finite values.
Results may differ from a plain program's by a relative error of at most 0.033.
Values may be sent and summed in bfloat16 or wider, within the bound.
A program may use at most 128 MiB of HBM per device.

v0:
```python
import jax
import jax.numpy as jnp
from jax import lax
from jax.sharding import PartitionSpec as P


def hidden_math(h_gate, h_up, d_act):
    sigmoid_gate = jax.nn.sigmoid(h_gate)
    act = (h_gate * sigmoid_gate * h_up).astype(jnp.bfloat16)
    d_gate = (d_act * h_up * sigmoid_gate * (1.0 + h_gate * (1.0 - sigmoid_gate))).astype(
        jnp.bfloat16
    )
    d_up = (d_act * h_gate * sigmoid_gate).astype(jnp.bfloat16)
    return (act, d_gate, d_up)


def contract_rows(left, right):
    return lax.dot_general(
        left, right, (((0,), (0,)), ((), ())), preferred_element_type=jnp.float32
    )


def contract_cols(left, right):
    return lax.dot_general(
        left, right, (((1,), (1,)), ((), ())), preferred_element_type=jnp.float32
    )


def on_device(tokens, cotangent, routes, gate_values, w_gate, w_up, w_down):
    tok_rows = tokens.shape[0]
    col_width = tokens.shape[1]
    top_count = routes.shape[1]
    experts = lax.axis_size("tok")
    capacity = min(tok_rows, tok_rows * top_count * 5 // (3 * experts))
    slot_total = experts * capacity
    flat_routes = routes.reshape(-1)
    onehot = (flat_routes[:, None] == jnp.arange(experts, dtype=jnp.int32)[None, :]).astype(
        jnp.int32
    )
    ranks = jnp.sum((jnp.cumsum(onehot, axis=0) - 1) * onehot, axis=1)
    slot_ids = (flat_routes * capacity + ranks).reshape(tok_rows, top_count)
    chosen = slot_ids[:, :, None] == jnp.arange(slot_total, dtype=jnp.int32)[None, None, :]
    placing = jnp.any(chosen, axis=1).astype(jnp.bfloat16)
    slot_gates = jnp.sum(jnp.where(chosen, gate_values[:, :, None], 0.0), axis=(0, 1)).reshape(
        experts, capacity
    )
    x_send = (
        contract_rows(placing, tokens).astype(jnp.bfloat16).reshape(experts, capacity, col_width)
    )
    dy_send = (
        contract_rows(placing, cotangent).astype(jnp.bfloat16).reshape(experts, capacity, col_width)
    )
    x_recv, dy_recv, gate_recv = (
        lax.all_to_all(x_send, "tok", split_axis=0, concat_axis=0, tiled=True),
        lax.all_to_all(dy_send, "tok", split_axis=0, concat_axis=0, tiled=True),
        lax.all_to_all(
            slot_gates.astype(jnp.bfloat16), "tok", split_axis=0, concat_axis=0, tiled=True
        ).astype(slot_gates.dtype),
    )
    x_rows = x_recv.reshape(slot_total, col_width)
    dy_rows = dy_recv.reshape(slot_total, col_width)
    gate_rows = gate_recv.reshape(slot_total)
    scaled = (dy_rows.astype(jnp.float32) * gate_rows[:, None]).astype(jnp.bfloat16)
    gate_mat = w_gate[0]
    up_mat = w_up[0]
    down_mat = w_down[0]
    part_gate = jnp.dot(x_rows, gate_mat, preferred_element_type=jnp.float32)
    part_up = jnp.dot(x_rows, up_mat, preferred_element_type=jnp.float32)
    part_down = contract_cols(scaled, down_mat)
    full_gate, full_up, full_down = (
        lax.psum(part_gate.astype(jnp.bfloat16), "exp").astype(jnp.float32),
        lax.psum(part_up.astype(jnp.bfloat16), "exp").astype(jnp.float32),
        lax.psum(part_down.astype(jnp.bfloat16), "exp").astype(jnp.float32),
    )
    act, d_gate, d_up = hidden_math(full_gate, full_up, full_down)
    down_grad = contract_rows(act, scaled).astype(jnp.bfloat16)
    gate_grad = contract_rows(x_rows, d_gate).astype(jnp.bfloat16)
    up_grad = contract_rows(x_rows, d_up).astype(jnp.bfloat16)
    contrib = (contract_cols(d_gate, gate_mat) + contract_cols(d_up, up_mat)).astype(jnp.bfloat16)
    contrib = contrib.reshape(experts, capacity, col_width)
    returned = lax.all_to_all(contrib, "tok", split_axis=0, concat_axis=0, tiled=True).reshape(
        slot_total, col_width
    )
    token_grad = jnp.dot(placing, returned, preferred_element_type=jnp.float32).astype(jnp.bfloat16)
    return (token_grad, gate_grad[None], up_grad[None], down_grad[None])


def solution(mesh):
    placed = (
        P("tok", "exp"),
        P("tok", "exp"),
        P("tok", None),
        P("tok", None),
        P("tok", "exp", None),
        P("tok", "exp", None),
        P("tok", None, "exp"),
    )
    return jax.shard_map(
        on_device,
        mesh=mesh,
        in_specs=placed,
        out_specs=(
            P("tok", "exp"),
            P("tok", "exp", None),
            P("tok", "exp", None),
            P("tok", None, "exp"),
        ),
        check_vma=False,
    )
```

profile of v0, /device:TPU:24, one launch (start us, length us, event | category | flops | bytes accessed | tf_op | source)
XLA Modules:
  0.0 300.5 jit_solution(8453458851491491316)
XLA Ops:
  8.4 1.7 reduce-window.6
  11.4 1.2 select_reduce_fusion
  13.4 11.5 %all-to-all-start.1 = ((bf16[32,1,40]{2,1,0:T(2,128)(2,1)}), bf16[32,1,40]{2,1,0:T(2,128)(2,1)S(1)}, u32[]{:S(2)}, u32[]{:S(2)}) async-start(bf16[32,1,40]{2,1,0:T(2,128)(2,1)} %convert_element_type.132), calls=%async_computation.1 | async-start | bytes 32768 | tf_op jit(solution)/shard_map/all_to_all | solution.py:56
  25.6 2.8 convolution_convert_fusion.3
  28.3 4.4 %all-to-all-done.1 = bf16[32,1,40]{2,1,0:T(2,128)(2,1)S(1)} async-done(((bf16[32,1,40]{2,1,0:T(2,128)(2,1)}), bf16[32,1,40]{2,1,0:T(2,128)(2,1)S(1)}, u32[]{:S(2)}, u32[]{:S(2)}) %all-to-all-start.1) | async-done | bytes 2592 | tf_op jit(solution)/shard_map/all_to_all | solution.py:56
  32.7 5.9 %all-to-all-start.2 = ((bf16[32,40,640]{2,1,0:T(8,128)(2,1)}), bf16[32,40,640]{2,1,0:T(8,128)(2,1)S(1)}, u32[]{:S(2)}, u32[]{:S(2)}) async-start(bf16[32,40,640]{2,1,0:T(8,128)(2,1)} %bitcast.5), calls=%async_computation.2 | async-start | bytes 3276800 | tf_op jit(solution)/shard_map/all_to_all | solution.py:54
  38.6 1.8 convolution_convert_fusion.4
  40.4 35.8 %all-to-all-done.2 = bf16[32,40,640]{2,1,0:T(8,128)(2,1)S(1)} async-done(((bf16[32,40,640]{2,1,0:T(8,128)(2,1)}), bf16[32,40,640]{2,1,0:T(8,128)(2,1)S(1)}, u32[]{:S(2)}, u32[]{:S(2)}) %all-to-all-start.2) | async-done | bytes 1638432 | tf_op jit(solution)/shard_map/all_to_all | solution.py:54
  77.4 7.7 %all-to-all-start = ((bf16[32,40,640]{2,1,0:T(8,128)(2,1)}), bf16[32,40,640]{2,1,0:T(8,128)(2,1)S(1)}, u32[]{:S(2)}, u32[]{:S(2)}) async-start(bf16[32,40,640]{2,1,0:T(8,128)(2,1)} %bitcast.62), calls=%async_computation | async-start | bytes 3276800 | tf_op jit(solution)/shard_map/all_to_all | solution.py:55
  85.4 5.3 %convolution_convert_fusion = bf16[1280,1024]{1,0:T(8,128)(2,1)} fusion(bf16[1280,640]{1,0:T(8,128)(2,1)} %bitcast.63, bf16[1,640,1024]{2,1,0:T(8,128)(2,1)S(1)} %copy-done), kind=kOutput, calls=%fused_computation.19 | convolution fusion | flops 1679032320 | bytes 5570560 | tf_op jit(solution)/shard_map/dot_general | solution.py:67
  90.7 3.7 %convolution_convert_fusion.1 = bf16[1280,1024]{1,0:T(8,128)(2,1)} fusion(bf16[1280,640]{1,0:T(8,128)(2,1)S(1)} %bitcast.65, bf16[1,640,1024]{2,1,0:T(8,128)(2,1)S(1)} %copy-done.12), kind=kOutput, calls=%fused_computation.20 | convolution fusion | flops 1679032320 | bytes 5570560 | tf_op jit(solution)/shard_map/dot_general | solution.py:68
  94.4 28.8 %all-to-all-done = bf16[32,40,640]{2,1,0:T(8,128)(2,1)S(1)} async-done(((bf16[32,40,640]{2,1,0:T(8,128)(2,1)}), bf16[32,40,640]{2,1,0:T(8,128)(2,1)S(1)}, u32[]{:S(2)}, u32[]{:S(2)}) %all-to-all-start) | async-done | bytes 1638432 | tf_op jit(solution)/shard_map/all_to_all | solution.py:55
  124.5 3.7 %convolution_convert_fusion.2 = bf16[1280,1024]{1,0:T(8,128)(2,1)} fusion(bf16[1280,640]{1,0:T(8,128)(2,1)S(1)} %bitcast.68, bf16[1,1024,640]{2,1,0:T(8,128)(2,1)S(1)} %copy-done.11), kind=kOutput, calls=%fused_computation.21 | convolution fusion | flops 1679032320 | bytes 5570560 | tf_op jit(solution)/shard_map/dot_general | solution.py:24
  128.3 103.5 %all-reduce.3.cloned.1.call-done = (bf16[1280,1024]{1,0:T(8,128)(2,1)}, bf16[1280,1024]{1,0:T(8,128)(2,1)}, bf16[1280,1024]{1,0:T(8,128)(2,1)}) async-done(((bf16[1280,1024]{1,0:T(8,128)(2,1)}, bf16[1280,1024]{1,0:T(8,128)(2,1)}, bf16[1280,1024]{1,0:T(8,128)(2,1)}), (bf16[1280,1024]{1,0:T(8,128)(2,1)}, bf16[1280,1024]{1,0:T(8,128)(2,1)}, bf16[1280,1024]{1,0:T(8,128)(2,1)})) %all-reduce.3.cloned.1.call-update) | async-done | bytes 7864336 | tf_op jit(solution)/shard_map/psum | solution.py:72
  231.7 4.9 %fusion.9 = (bf16[1280,1024]{1,0:T(8,128)(2,1)S(1)}, bf16[1280,1024]{1,0:T(8,128)(2,1)S(1)}) fusion(bf16[1280,1024]{1,0:T(8,128)(2,1)} %get-tuple-element.6, bf16[1280,1024]{1,0:T(8,128)(2,1)} %get-tuple-element.5, bf16[1280,1024]{1,0:T(8,128)(2,1)} %get-tuple-element.4), kind=kLoop, calls=%fused_computation.15 | loop fusion | flops 20971520 | bytes 13107200 | tf_op jit(solution)/shard_map/convert_element_type | solution.py:13
  236.7 2.2 fusion.23
  239.0 3.6 %fusion.12 = bf16[1280,640]{1,0:T(8,128)(2,1)} fusion(f32[1280,640]{1,0:T(8,128)S(1)} %fusion.23, bf16[1280,1024]{1,0:T(8,128)(2,1)S(1)} %get-tuple-element.7, bf16[1,640,1024]{2,1,0:T(8,128)(2,1)S(1)} %copy-done.13), kind=kOutput, calls=%fused_computation.26 | convolution fusion | flops 1679360000 | bytes 8847360 | tf_op jit(solution)/shard_map/dot_general | solution.py:24
  242.6 10.2 %all-to-all-start.3 = ((bf16[32,40,640]{2,1,0:T(8,128)(2,1)}), bf16[32,40,640]{2,1,0:T(8,128)(2,1)}, u32[]{:S(2)}, u32[]{:S(2)}) async-start(bf16[32,40,640]{2,1,0:T(8,128)(2,1)} %bitcast.67), calls=%async_computation.3 | async-start | bytes 3276800 | tf_op jit(solution)/shard_map/all_to_all | solution.py:81
  253.3 1.4 copy-done.6
  254.7 4.5 %fusion.19 = bf16[1,640,1024]{2,1,0:T(8,128)(2,1)} fusion(bf16[1280,640]{1,0:T(8,128)(2,1)} %bitcast.64, bf16[1280,1024]{1,0:T(8,128)(2,1)S(1)} %copy-done.6), kind=kOutput, calls=%fused_computation.34 | convolution fusion | flops 1678376960 | bytes 5570560 | tf_op jit(solution)/shard_map/dot_general | solution.py:18
  259.2 3.0 fusion.18
  262.2 3.9 %fusion.20 = bf16[1,1024,640]{2,1,0:T(8,128)(2,1)} fusion(bf16[1280,640]{1,0:T(8,128)(2,1)S(1)} %fusion.11, bf16[1280,1024]{1,0:T(8,128)(2,1)S(1)} %copy-done.1, bf16[1280,1024]{1,0:T(8,128)(2,1)S(1)} %copy-done.2), kind=kOutput, calls=%fused_computation.35 | convolution fusion | flops 1688862720 | bytes 8192000 | tf_op jit(solution)/shard_map/dot_general | solution.py:18
  266.1 25.1 %all-to-all-done.3 = bf16[32,40,640]{2,1,0:T(8,128)(2,1)} async-done(((bf16[32,40,640]{2,1,0:T(8,128)(2,1)}), bf16[32,40,640]{2,1,0:T(8,128)(2,1)}, u32[]{:S(2)}, u32[]{:S(2)}) %all-to-all-start.3) | async-done | bytes 1638432 | tf_op jit(solution)/shard_map/all_to_all | solution.py:81
  291.1 2.5 convolution_convert_fusion.7
  (46 shorter events, 7.1 us)
Async XLA Ops:
  7.2 78.2 %copy-start = (bf16[1,640,1024]{2,1,0:T(8,128)(2,1)S(1)}, bf16[1,640,1024]{2,1,0:T(8,128)(2,1)}, u32[]{:S(2)}) copy-start(bf16[1,640,1024]{2,1,0:T(8,128)(2,1)} %param.11) | copy-start | bytes 3932164
  13.4 19.4 %all-to-all-start.1 = ((bf16[32,1,40]{2,1,0:T(2,128)(2,1)}), bf16[32,1,40]{2,1,0:T(2,128)(2,1)S(1)}, u32[]{:S(2)}, u32[]{:S(2)}) async-start(bf16[32,1,40]{2,1,0:T(2,128)(2,1)} %convert_element_type.132), calls=%async_computation.1 | async-start | bytes 32768 | tf_op jit(solution)/shard_map/all_to_all | solution.py:56
  25.6 13.0 %copy-start.10 = (bf16[128,640]{1,0:T(8,128)(2,1)S(1)}, bf16[128,640]{1,0:T(8,128)(2,1)}, u32[]{:S(2)}) copy-start(bf16[128,640]{1,0:T(8,128)(2,1)} %param.8) | copy-start | bytes 491524
  32.7 43.5 %all-to-all-start.2 = ((bf16[32,40,640]{2,1,0:T(8,128)(2,1)}), bf16[32,40,640]{2,1,0:T(8,128)(2,1)S(1)}, u32[]{:S(2)}, u32[]{:S(2)}) async-start(bf16[32,40,640]{2,1,0:T(8,128)(2,1)} %bitcast.5), calls=%async_computation.2 | async-start | bytes 3276800 | tf_op jit(solution)/shard_map/all_to_all | solution.py:54
  76.2 1.2 copy-start.7
  77.4 45.9 %all-to-all-start = ((bf16[32,40,640]{2,1,0:T(8,128)(2,1)}), bf16[32,40,640]{2,1,0:T(8,128)(2,1)S(1)}, u32[]{:S(2)}, u32[]{:S(2)}) async-start(bf16[32,40,640]{2,1,0:T(8,128)(2,1)} %bitcast.62), calls=%async_computation | async-start | bytes 3276800 | tf_op jit(solution)/shard_map/all_to_all | solution.py:55
  85.1 146.6 %all-reduce.3.cloned.1.call-start = ((), (), s32[]{:S(2)}) async-start(), calls=%async_computation.4 | async-start | bytes 15728640 | tf_op jit(solution)/shard_map/psum | solution.py:72
  85.4 5.4 %copy-start.8 = (bf16[32,40,640]{2,1,0:T(8,128)(2,1)S(1)}, bf16[32,40,640]{2,1,0:T(8,128)(2,1)}, u32[]{:S(2)}) copy-start(bf16[32,40,640]{2,1,0:T(8,128)(2,1)} %copy-done.7) | copy-start | bytes 4915204
  85.4 5.3 %copy-start.12 = (bf16[1,640,1024]{2,1,0:T(8,128)(2,1)S(1)}, bf16[1,640,1024]{2,1,0:T(8,128)(2,1)}, u32[]{:S(2)}) copy-start(bf16[1,640,1024]{2,1,0:T(8,128)(2,1)} %param.12) | copy-start | bytes 3932164
  123.2 1.3 copy-start.11
  236.7 2.3 copy-start.3
  236.7 2.3 copy-start.5
  236.7 2.3 copy-start.13
  242.6 48.6 %all-to-all-start.3 = ((bf16[32,40,640]{2,1,0:T(8,128)(2,1)}), bf16[32,40,640]{2,1,0:T(8,128)(2,1)}, u32[]{:S(2)}, u32[]{:S(2)}) async-start(bf16[32,40,640]{2,1,0:T(8,128)(2,1)} %bitcast.67), calls=%async_computation.3 | async-start | bytes 3276800 | tf_op jit(solution)/shard_map/all_to_all | solution.py:81
  252.9 1.7 copy-start.6
  254.7 4.6 %copy-start.4 = (bf16[1280,1024]{1,0:T(8,128)(2,1)S(1)}, bf16[1280,1024]{1,0:T(8,128)(2,1)}, u32[]{:S(2)}) copy-start(bf16[1280,1024]{1,0:T(8,128)(2,1)} %copy-done.3) | copy-start | bytes 7864324
  254.7 4.6 %copy-start.9 = (bf16[32,40,640]{2,1,0:T(8,128)(2,1)S(1)}, bf16[32,40,640]{2,1,0:T(8,128)(2,1)}, u32[]{:S(2)}) copy-start(bf16[32,40,640]{2,1,0:T(8,128)(2,1)} %copy-done.7) | copy-start | bytes 4915204
  259.2 3.0 copy-start.1
  259.2 3.0 copy-start.2
Sparse Core Ops, SparseCore 0:
  128.4 103.2 all-reduce.2
where the time goes:
time: 303 us; the launch traced here: 301 us
  waiting for transfers between devices  198 us (65%)
  matrix products  37.1 us (12%)
  starting transfers between devices  35.5 us (12%)
  between operations  14.3 us (5%)
  other arithmetic  10.2 us (3%)
  local copies, waits for them, and re-layouts  6 us (2%)
    psum x1, waiting for transfers between devices, on_device(): lax.psum(part_up.astype(jnp.bfloat16), 'exp').astype(jnp.float32)  103 us
    all_to_all x1, waiting for transfers between devices, on_device(): lax.all_to_all(x_send, 'tok', split_axis=0, concat_axis=0, tiled=True)  35.8 us
    all_to_all x1, waiting for transfers between devices, on_device(): lax.all_to_all(dy_send, 'tok', split_axis=0, concat_axis=0, tiled=True)  28.8 us
    all_to_all x1, waiting for transfers between devices, on_device(): lax.all_to_all(contrib, 'tok', split_axis=0, concat_axis=0, tiled=True)  25.1 us
    dot_general x5, matrix products, contract_rows(): lax.dot_general(left, right, (((0,), (0,)), ((), ())), preferred_element_...  16 us
    all_to_all x1, starting transfers between devices, on_device(): lax.all_to_all(slot_gates.astype(jnp.bfloat16), 'tok', split_axis=0, conc...  11.5 us
    all_to_all x1, starting transfers between devices, on_device(): lax.all_to_all(contrib, 'tok', split_axis=0, concat_axis=0, tiled=True)  10.2 us
    dot_general x3, matrix products, contract_cols(): lax.dot_general(left, right, (((1,), (1,)), ((), ())), preferred_element_...  9.52 us
  transfers between devices with their start and end apart: 5, of which 5 were waited for; matrix products, arithmetic and copies ran while one was open for 9% of the time, Pallas kernels for 0%

commit v1 on v0

v1 whole, which is shorter than its diff:
```python
import jax
import jax.numpy as jnp
from jax import lax
from jax.experimental import pallas as pl
from jax.experimental.pallas import tpu as pltpu
from jax.sharding import PartitionSpec as P

MESH = pl.DeviceIdType.MESH
F32, BF16 = jnp.float32, jnp.bfloat16

NY, NZ, NX, NC = 4, 8, 4, 2
T = 128
CAP = 40
W = 640
FF = 1024
SH = FF // (NX * NC)
PAIRS = ((0, 1), (3, -3), (4, -2), (2, -1))
PLACE = {off: (c, i) for c, pair in enumerate(PAIRS) for i, off in enumerate(pair)}
YOFF = (0, 1, -1, 2)
YINV = (0, 2, 1, 3)
NCH = len(PAIRS)
NU = 2 * NCH
HALF = 2 * CAP
ROWS = 2 * HALF
DEPTH = 6


def dot(a, b):
    return jnp.dot(a, b, preferred_element_type=F32)


def dot_nt(a, b):
    return lax.dot_general(a, b, (((1,), (1,)), ((), ())), preferred_element_type=F32)


def dot_tn(a, b):
    return lax.dot_general(a, b, (((0,), (0,)), ((), ())), preferred_element_type=F32)


def kernel(
    tok_ref, cot_ref, info_ref, wg_hbm, wu_hbm, wd_hbm,
    tg_ref, gg_hbm, ug_hbm, dg_hbm,
    wg, wu, wd, gg, ug, dg, infob, zx, zd, p2, grow,
    ysx, yss, xr, sr, hp, cr, q, t1, t2, gb, cs, yr, zs, zr, xt,
    info_s, info_r, zx_s, zx_r, zd_s, zd_r, yx_s, yx_r, ys_s, ys_r,
    c1_s, c1_r, x1_s, x1_r, x2_s, x2_r, ag_s, ag_r, cg_s, cg_r,
    yr_s, yr_r, zr_s, zr_r, w_sem, o_sem,
):
    tok = lax.axis_index("tok")
    exp = lax.axis_index("exp")
    y, z = tok // NZ, lax.rem(tok, NZ)
    x, core = exp // NC, lax.rem(exp, NC)

    def at_z(off):
        return (y * NZ + lax.rem(z + off + NZ, NZ), exp)

    def at_y(off):
        return (lax.rem(y + off + NY, NY) * NZ + z, exp)

    def col(off):
        return lax.rem(x + off + NX, NX)

    def at_x(off):
        return (tok, col(off) * NC + core)

    sibling = (tok, x * NC + (1 - core))

    def rc(src, dst, s, r, dev):
        return pltpu.make_async_remote_copy(
            src_ref=src, dst_ref=dst, send_sem=s, recv_sem=r, device_id=dev, device_id_type=MESH
        )

    def info_copy(off):
        return rc(info_ref, infob.at[(NZ - off) % NZ], info_s.at[off], info_r.at[off], at_z(off))

    def z_copy(buf, own, ss, rs, off):
        step = 1 if off > 0 else -1
        before = off - step
        if before == 0:
            src = own
        else:
            src = buf.at[PLACE[before][0], PLACE[before][1]]
        c, i = PLACE[off if off in PLACE else off + NZ]
        k = (off + NZ) % NZ
        return rc(src, buf.at[c, i], ss.at[k], rs.at[k], at_z(-step))

    def zx_copy(off):
        return z_copy(zx, tok_ref, zx_s, zx_r, off)

    def zd_copy(off):
        return z_copy(zd, cot_ref, zd_s, zd_r, off)

    def y_copy(stage, buf, ss, rs, c, k):
        j = YINV[k]
        return rc(stage.at[c, k - 1], buf.at[2 * c + j // 2, j % 2], ss.at[c, k], rs.at[c, j], at_y(YOFF[k]))

    def yx_copy(c, k):
        return y_copy(ysx, xr, yx_s, yx_r, c, k)

    def ys_copy(c, k):
        return y_copy(yss, sr, ys_s, ys_r, c, k)

    def ret_copy(c, k):
        j = YINV[k]
        return rc(
            cs.at[2 * c + k // 2, k % 2], yr.at[2 * c + j // 2, j % 2], yr_s.at[c, k], yr_r.at[c, j], at_y(YOFF[k])
        )

    def c1_copy(u):
        return rc(hp.at[u, 1 - core], cr.at[u], c1_s.at[u], c1_r.at[u], sibling)

    def x1_copy(u, n):
        src, dst, to = (
            (q.at[u, 2, 0], t1.at[u, 0], 1),
            (q.at[u, 2, 1], t1.at[u, 1], -1),
            (q.at[u, 1, 1], t2.at[u, 0, 1], 1),
            (q.at[u, 3, 0], t2.at[u, 1, 0], -1),
        )[n]
        return rc(src, dst, x1_s.at[u, n], x1_r.at[u, n], at_x(to))

    def x2_copy(u, n):
        src, dst, to = ((q.at[u, 1, 0], t2.at[u, 0, 0], 1), (q.at[u, 3, 1], t2.at[u, 1, 1], -1))[n]
        return rc(src, dst, x2_s.at[u, n], x2_r.at[u, n], at_x(to))

    def ag_send(u, n):
        part, to = (
            (gb.at[u, core, x], 1),
            (gb.at[u, core, x], -1),
            (gb.at[u, core, col(-1), 0], 1),
            (gb.at[u, core, col(1), 1], -1),
        )[n]
        return rc(part, part, ag_s.at[u, n], ag_r.at[u, n], at_x(to))

    def ag_wait(u, n):
        part = (
            gb.at[u, core, col(-1)],
            gb.at[u, core, col(1)],
            gb.at[u, core, col(2), 0],
            gb.at[u, core, col(2), 1],
        )[n]
        rc(part, part, ag_s.at[u, n], ag_r.at[u, n], at_x(1)).wait_recv()

    SHARDS = (0, -1, 1, 2)

    def cg_send(u, n):
        part = gb.at[u, core, col(SHARDS[n])]
        return rc(part, part, cg_s.at[u, n], cg_r.at[u, n], sibling)

    def cg_wait(u, n):
        part = gb.at[u, 1 - core, col(SHARDS[n])]
        rc(part, part, cg_s.at[u, n], cg_r.at[u, n], sibling).wait_recv()

    def zr_copy(c, i):
        off = PAIRS[c][i]
        return rc(zs.at[c, i], zr.at[c, i], zr_s.at[c, i], zr_r.at[c, i], at_z(off))

    weights = [
        pltpu.make_async_copy(src, dst, w_sem.at[n])
        for n, (src, dst) in enumerate(((wg_hbm, wg), (wu_hbm, wu), (wd_hbm, wd)))
    ]
    for copy in weights:
        copy.start()
    barrier = pltpu.get_barrier_semaphore()
    partners = [at_z(off) for off in range(1, NZ)] + [at_y(off) for off in (1, -1, 2)]
    partners += [at_x(1), at_x(-1), sibling]
    for dev in partners:
        pl.semaphore_signal(barrier, inc=1, device_id=dev, device_id_type=MESH)
    pl.semaphore_wait(barrier, len(partners))

    for off in range(1, NZ):
        info_copy(off).start()
    for off in (1, -1):
        zx_copy(off).start()
    for off in (1, -1):
        zd_copy(off).start()
    zx[0, 0] = tok_ref[...]
    zd[0, 0] = cot_ref[...]
    infob[0] = info_ref[...]
    for off in range(1, NZ):
        info_copy(off).wait_recv()

    before = (
        lax.broadcasted_iota(jnp.int32, (T, T), 0) < lax.broadcasted_iota(jnp.int32, (T, T), 1)
    ).astype(BF16)
    masks, gates = [], []
    for off in range(NZ):
        block = infob[off]
        ids, vals = block[0:8], block[8:16]
        for k in range(NY):
            expert = (lax.rem(y + YOFF[k] + NY, NY) * NZ + z).astype(F32)
            hit = ids == expert
            masks.append(jnp.sum(jnp.where(hit, 1.0, 0.0), axis=0, keepdims=True))
            gates.append(jnp.sum(jnp.where(hit, vals, 0.0), axis=0, keepdims=True))
    mask_all = jnp.concatenate(masks, axis=0)
    rank_all = dot(mask_all.astype(BF16), before)
    want = lax.broadcasted_iota(jnp.int32, (CAP, T), 0).astype(F32)
    nothing = jnp.zeros((CAP, T), F32)
    for c in range(NCH):
        tables, gcols = [], []
        for k in range(NY):
            for i in range(2):
                n = (PAIRS[c][i] % NZ) * NY + k
                on = (rank_all[n : n + 1] == want) & (mask_all[n : n + 1] > 0.5)
                table = jnp.where(on, 1.0, 0.0)
                gcols.append(jnp.sum(jnp.where(on, gates[n], 0.0), axis=1, keepdims=True))
                tables.append(jnp.concatenate([table, nothing] if i == 0 else [nothing, table], axis=1))
        p2[c] = jnp.concatenate(tables, axis=0).astype(BF16)
        grow[c] = jnp.concatenate(gcols, axis=0)

    def place_x(c):
        rows = dot(p2[c], zx[c].reshape(2 * T, W)).astype(BF16)
        xr[2 * c, 0] = rows[:HALF]
        for k in (1, 2, 3):
            ysx[c, k - 1] = rows[k * HALF : (k + 1) * HALF]
            yx_copy(c, k).start()

    def place_s(c):
        rows = (dot(p2[c], zd[c].reshape(2 * T, W)) * grow[c]).astype(BF16)
        sr[2 * c, 0] = rows[:HALF]
        for k in (1, 2, 3):
            yss[c, k - 1] = rows[k * HALF : (k + 1) * HALF]
            ys_copy(c, k).start()

    def pass_on(copy, d):
        for off in (d, -d):
            copy(off).wait_recv()
        for off in (d + 1, -d - 1):
            if d < 3 or (off > 0) == (copy is zx_copy):
                copy(off).start()

    pass_on(zx_copy, 1)
    place_x(0)
    pass_on(zd_copy, 1)
    place_s(0)
    for copy in weights:
        copy.wait()

    def y_wait(copy, u):
        c, h = u // 2, lax.rem(u, 2)

        @pl.when(h == 0)
        def _():
            copy(c, YINV[1]).wait_recv()

        @pl.when(h == 1)
        def _():
            copy(c, YINV[2]).wait_recv()
            copy(c, YINV[3]).wait_recv()

    def partial(u, a, value):
        value = value.astype(BF16)
        for s in range(NX * NC):
            hp[u, s % NC, a, s // NC] = value[:, s * SH : (s + 1) * SH]

    def s0(u):
        y_wait(yx_copy, u)
        rows = xr[u].reshape(ROWS, W)
        partial(u, 0, dot(rows, wg[...]))
        partial(u, 1, dot(rows, wu[...]))
        y_wait(ys_copy, u)
        partial(u, 2, dot_nt(sr[u].reshape(ROWS, W), wd[...]))
        c1_copy(u).start()

    def s1(u):
        c1_copy(u).wait_recv()
        for j in (2, 1, 3, 0):
            xx = col(j)
            for a in range(3):
                value = (hp[u, core, a, xx].astype(F32) + cr[u, a, xx].astype(F32)).astype(BF16)
                q[u, j, 0, a] = value[:HALF]
                q[u, j, 1, a] = value[HALF:]
            if j == 2:
                x1_copy(u, 0).start()
                x1_copy(u, 1).start()
            elif j == 1:
                x1_copy(u, 2).start()
            elif j == 3:
                x1_copy(u, 3).start()

    def s2(u):
        for n, (j, half) in enumerate(((1, 0), (3, 1))):
            x1_copy(u, n).wait_recv()
            q[u, j, half] = (q[u, j, half].astype(F32) + t1[u, n].astype(F32)).astype(BF16)
            x2_copy(u, n).start()

    def s3(u):
        x1_copy(u, 2).wait_recv()
        x1_copy(u, 3).wait_recv()
        x2_copy(u, 0).wait_recv()
        x2_copy(u, 1).wait_recv()
        for half in range(2):
            h = q[u, 0, half].astype(F32) + t2[u, 0, half].astype(F32) + t2[u, 1, half].astype(F32)
            h_gate, h_up, d_act = h[0], h[1], h[2]
            sigma = 1.0 / (1.0 + jnp.exp(-h_gate))
            gb[u, core, x, half, 0] = (h_gate * sigma * h_up).astype(BF16)
            gb[u, core, x, half, 1] = (d_act * h_up * sigma * (1.0 + h_gate * (1.0 - sigma))).astype(BF16)
            gb[u, core, x, half, 2] = (d_act * h_gate * sigma).astype(BF16)
        ag_send(u, 0).start()
        ag_send(u, 1).start()
        cg_send(u, 0).start()

    def s4(u):
        ag_wait(u, 0)
        ag_send(u, 2).start()
        ag_wait(u, 1)
        ag_send(u, 3).start()
        cg_send(u, 1).start()
        cg_send(u, 2).start()

    def s5(u):
        ag_wait(u, 2)
        ag_wait(u, 3)
        cg_send(u, 3).start()

    def hidden(u, a):
        return jnp.concatenate(
            [gb[u, s % NC, s // NC, :, a].reshape(ROWS, SH) for s in range(NX * NC)], axis=1
        )

    def s6(u):
        for n in range(4):
            cg_wait(u, n)
        value = (dot_nt(hidden(u, 1), wg[...]) + dot_nt(hidden(u, 2), wu[...])).astype(BF16)
        cs[u, 0] = value[:HALF]
        cs[u, 1] = value[HALF:]
        c, h = u // 2, lax.rem(u, 2)

        @pl.when(h == 0)
        def _():
            yr[u, 0] = value[:HALF]
            ret_copy(c, 1).start()

        @pl.when(h == 1)
        def _():
            ret_copy(c, 2).start()
            ret_copy(c, 3).start()

    def s7(c):
        for k in (1, 2, 3):
            ret_copy(c, k).wait_recv()
        rows = yr[2 * c : 2 * c + 2].reshape(2 * ROWS, W)
        value = dot_tn(p2[c], rows).astype(BF16)
        for i in range(2):
            if PAIRS[c][i] == 0:
                zr[c, i] = value[i * T : (i + 1) * T]
            else:
                zs[c, i] = value[i * T : (i + 1) * T]
                zr_copy(c, i).start()

    def step(s, carry):
        for k, stage in ((5, s5), (4, s4), (3, s3), (2, s2), (1, s1)):

            @pl.when((s >= k) & (s < NU + k))
            def _(k=k, stage=stage):
                stage(s - k)

        @pl.when(s < NU)
        def _():
            s0(s)

        @pl.when((s >= DEPTH) & (s < NU + DEPTH))
        def _():
            s6(s - DEPTH)

        for c in range(NCH - 1):

            @pl.when(s == 2 * c + DEPTH + 2)
            def _(c=c):
                s7(c)

        @pl.when(s == 0)
        def _():
            pass_on(zx_copy, 2)
            pass_on(zd_copy, 2)

        @pl.when(s == 1)
        def _():
            pass_on(zx_copy, 3)
            pass_on(zd_copy, 3)

        @pl.when(s == 2)
        def _():
            zx_copy(4).wait_recv()
            zd_copy(-4).wait_recv()

        for c in range(1, NCH):

            @pl.when(s == 2 * c - 1)
            def _(c=c):
                place_x(c)
                place_s(c)

        return carry

    lax.fori_loop(0, NU + DEPTH, step, 0)

    everything = xr[...].reshape(NU * ROWS, W)
    for n in range(W // 128):
        xt[n * 128 : (n + 1) * 128] = everything[:, n * 128 : (n + 1) * 128].T

    def all_rows(xx, a):
        return jnp.concatenate(
            [gb[:, cc, xx, :, a].reshape(NU * ROWS, SH) for cc in range(NC)], axis=1
        )

    def gate_step(xx, carry):
        at = pl.ds(pl.multiple_of(xx * 2 * SH, 2 * SH), 2 * SH)
        gg[:, at] = dot(xt[...], all_rows(xx, 1)).astype(BF16)
        return carry

    lax.fori_loop(0, NX, gate_step, 0)
    outs = [
        pltpu.make_async_copy(src, dst, o_sem.at[n])
        for n, (src, dst) in enumerate(((gg, gg_hbm), (ug, ug_hbm), (dg, dg_hbm)))
    ]
    outs[0].start()
    s7(NCH - 1)

    def rest_step(xx, carry):
        at = pl.ds(pl.multiple_of(xx * 2 * SH, 2 * SH), 2 * SH)
        ug[:, at] = dot(xt[...], all_rows(xx, 2)).astype(BF16)
        dg[at, :] = dot_tn(all_rows(xx, 0), sr[...].reshape(NU * ROWS, W)).astype(BF16)
        return carry

    lax.fori_loop(0, NX, rest_step, 0)
    outs[1].start()
    outs[2].start()

    total = zr[0, 0].astype(F32)
    for c in range(NCH):
        for i in range(2):
            if PAIRS[c][i] != 0:
                zr_copy(c, i).wait_recv()
                total = total + zr[c, i].astype(F32)
    tg_ref[...] = total.astype(BF16)

    for off in range(1, NZ):
        info_copy(off).wait_send()
    for d in (1, 2, 3):
        for off in (d, -d):
            zx_copy(off).wait_send()
            zd_copy(off).wait_send()
    zx_copy(4).wait_send()
    zd_copy(-4).wait_send()

    def drain_u(u, carry):
        c1_copy(u).wait_send()
        for n in range(4):
            x1_copy(u, n).wait_send()
            ag_send(u, n).wait_send()
            cg_send(u, n).wait_send()
        for n in range(2):
            x2_copy(u, n).wait_send()
        return carry

    def drain_c(c, carry):
        for k in (1, 2, 3):
            yx_copy(c, k).wait_send()
            ys_copy(c, k).wait_send()
            ret_copy(c, k).wait_send()
        return carry

    lax.fori_loop(0, NU, drain_u, 0)
    lax.fori_loop(0, NCH, drain_c, 0)
    for c in range(NCH):
        for i in range(2):
            if PAIRS[c][i] != 0:
                zr_copy(c, i).wait_send()
    for copy in outs:
        copy.wait()


def on_device(tokens, cotangent, routes, gate_values, w_gate, w_up, w_down):
    pad = ((0, 2), (0, 0))
    ids = jnp.pad(routes.astype(F32).T, pad, constant_values=-1.0)
    info = jnp.concatenate([ids, jnp.pad(gate_values.T, pad)], axis=0)
    sem = pltpu.SemaphoreType.DMA

    def vm(*shape, dtype=BF16):
        return pltpu.VMEM(shape, dtype)

    vmem = pl.BlockSpec(memory_space=pltpu.VMEM)
    hbm = pl.BlockSpec(memory_space=pl.ANY)
    scratch = [
        vm(W, FF), vm(W, FF), vm(FF, W),
        vm(W, FF), vm(W, FF), vm(FF, W),
        vm(NZ, 16, T, dtype=F32), vm(NCH, 2, T, W), vm(NCH, 2, T, W),
        vm(NCH, 2 * ROWS, 2 * T), vm(NCH, 2 * ROWS, 1, dtype=F32),
        vm(NCH, 3, HALF, W), vm(NCH, 3, HALF, W),
        vm(NU, 2, HALF, W), vm(NU, 2, HALF, W),
        vm(NU, NC, 3, NX, ROWS, SH), vm(NU, 3, NX, ROWS, SH),
        vm(NU, NX, 2, 3, HALF, SH), vm(NU, 2, 3, HALF, SH), vm(NU, 2, 2, 3, HALF, SH),
        vm(NU, NC, NX, 2, 3, HALF, SH),
        vm(NU, 2, HALF, W), vm(NU, 2, HALF, W),
        vm(NCH, 2, T, W), vm(NCH, 2, T, W),
        vm(W, NU * ROWS),
    ]
    sems = []
    for shape in ((NZ,), (NZ,), (NZ,), (NCH, 4), (NCH, 4), (NU,), (NU, 4), (NU, 2), (NU, 4), (NU, 4), (NCH, 4), (NCH, 2)):
        sems += [sem(shape), sem(shape)]
    sems += [sem((3,)), sem((3,))]
    flops = 2 * NU * ROWS * W * FF * 8
    token_grad, gate_grad, up_grad, down_grad = pl.pallas_call(
        kernel,
        out_shape=(
            jax.ShapeDtypeStruct((T, W), BF16),
            jax.ShapeDtypeStruct((W, FF), BF16),
            jax.ShapeDtypeStruct((W, FF), BF16),
            jax.ShapeDtypeStruct((FF, W), BF16),
        ),
        in_specs=[vmem, vmem, vmem, hbm, hbm, hbm],
        out_specs=(vmem, hbm, hbm, hbm),
        scratch_shapes=scratch + sems,
        compiler_params=pltpu.CompilerParams(
            collective_id=0, has_side_effects=True, vmem_limit_bytes=60 * 1024 * 1024
        ),
        cost_estimate=pl.CostEstimate(flops=flops, bytes_accessed=12_000_000, transcendentals=0),
    )(tokens, cotangent, info, w_gate[0], w_up[0], w_down[0])
    return (token_grad, gate_grad[None], up_grad[None], down_grad[None])


def solution(mesh):
    return jax.shard_map(
        on_device,
        mesh=mesh,
        in_specs=(
            P("tok", "exp"),
            P("tok", "exp"),
            P("tok", None),
            P("tok", None),
            P("tok", "exp", None),
            P("tok", "exp", None),
            P("tok", None, "exp"),
        ),
        out_specs=(
            P("tok", "exp"),
            P("tok", "exp", None),
            P("tok", "exp", None),
            P("tok", None, "exp"),
        ),
        check_vma=False,
    )
```

time: 303 us -> 143 us (0.47)
  waiting for transfers between devices: 198 us -> 0 us
  Pallas kernels: 0 us -> 131 us
  matrix products: 37.1 us -> 0 us
  starting transfers between devices: 35.5 us -> 0 us
  between operations: 14.3 us -> 0.64 us
  other arithmetic: 10.2 us -> 1.98 us
    pallas_call x0 -> x1, Pallas kernels: none -> 131 us  [on_device(): pl.pallas_call(kernel, out_shape=(jax.ShapeDtypeStruct((T, W), BF16), jax...]
    psum x1 -> x0, waiting for transfers between devices: 103 us -> none  [on_device(): lax.psum(part_up.astype(jnp.bfloat16), 'exp').astype(jnp.float32)]
    all_to_all x4 -> x0, waiting for transfers between devices: 94 us -> none  [the longest x1 35.8 us: on_device(): lax.all_to_all(x_send, 'tok', split_axis=0, concat_axis=0, tiled=True)]
    dot_general x11 -> x0, matrix products: 37.1 us -> none  [the longest x5 16 us: contract_rows(): lax.dot_general(left, right, (((0,), (0,)), ((), ())), preferred_element_...]
    all_to_all x4 -> x0, starting transfers between devices: 35.3 us -> none  [the longest x1 11.5 us: on_device(): lax.all_to_all(slot_gates.astype(jnp.bfloat16), 'tok', split_axis=0, conc...]
    convert_element_type x6 -> x0, other arithmetic: 5.67 us -> none  [the longest x1 4.91 us: hidden_math(): d_up = (d_act * h_gate * sigmoid_gate).astype(jnp.bfloat16)]
    unnamed x29 -> x8, local copies, waits for them, and re-layouts: 4.5 us -> 7.01 us
  transfers between devices with their start and end apart: 5 -> 0, of which waited for: 5 -> 0; matrix products, arithmetic and copies ran while one was open for 9% -> 0% of each run, Pallas kernels for 0% -> 0%
where the time goes in v1:
time: 143 us; the launch traced here: 141 us
  Pallas kernels  131 us (92%)
  local copies, waits for them, and re-layouts  7.01 us (5%)
  other arithmetic  1.98 us (1%)
    pallas_call x1, Pallas kernels, on_device(): pl.pallas_call(kernel, out_shape=(jax.ShapeDtypeStruct((T, W), BF16), jax...  131 us
    unnamed x8, local copies, waits for them, and re-layouts  7.01 us

profile of v1, /device:TPU:24, one launch (start us, length us, event | category | flops | bytes accessed | tf_op | source)
XLA Modules:
  0.0 140.6 jit_solution(17721101928350536205)
XLA Ops:
  0.6 0.7 convert_bitcast_fusion
  1.3 1.3 select_maximum_fusion.info_ref
  2.6 130.9 %shard_map.102 = (bf16[128,640]{1,0:T(8,128)(2,1)}, bf16[640,1024]{1,0:T(8,128)(2,1)}, bf16[640,1024]{1,0:T(8,128)(2,1)}, bf16[1024,640]{1,0:T(8,128)(2,1)}) custom-call(bf16[128,640]{1,0:T(8,128)(2,1)} %tok_ref.1, bf16[128,640]{1,0:T(8,128)(2,1)} %cot_ref.1, f32[16,128]{1,0:T(8,128)} %select_maximum_fusion.info_ref, bf16[640,1024]{1,0:T(8,128)(2,1)} %bitcast.13, ...), custom_call_target="tpu_custom_call" | custom-call | flops 13421772800 | bytes 12000000 | tf_op jit(solution)/shard_map/pallas_call | solution.py:503
  133.5 1.6 %copy.15 = bf16[128,640]{1,0:T(8,128)(2,1)} copy(bf16[128,640]{1,0:T(8,128)(2,1)} %get-tuple-element.16) | data formatting | bytes 327680
  135.1 0.0 copy-start.1
  135.1 2.6 %copy.16 = bf16[1,640,1024]{2,1,0:T(8,128)(2,1)} copy(bf16[1,640,1024]{2,1,0:T(8,128)(2,1)} %bitcast.11) | data formatting | bytes 2621440
  137.7 0.0 copy-done.1
  137.7 0.0 copy-start
  137.7 1.1 copy.17
  138.8 0.7 copy-done
  139.5 1.1 copy.18
Async XLA Ops:
  135.1 2.6 %copy-start.1 = (bf16[640,1024]{1,0:T(8,128)(2,1)S(1)}, bf16[640,1024]{1,0:T(8,128)(2,1)}, u32[]{:S(2)}) copy-start(bf16[640,1024]{1,0:T(8,128)(2,1)} %get-tuple-element.10) | copy-start | bytes 3932164
  137.7 1.8 %copy-start = (bf16[1024,640]{1,0:T(8,128)(2,1)S(1)}, bf16[1024,640]{1,0:T(8,128)(2,1)}, u32[]{:S(2)}) copy-start(bf16[1024,640]{1,0:T(8,128)(2,1)} %get-tuple-element.11) | copy-start | bytes 3932164

commit v2 on v0

v2 whole, which is shorter than its diff:
```python
import jax
import jax.numpy as jnp
from jax import lax
from jax.experimental import pallas as pl
from jax.experimental.pallas import tpu as pltpu
from jax.sharding import PartitionSpec as P

MESH = pl.DeviceIdType.MESH
F32, BF16 = jnp.float32, jnp.bfloat16

NY, NZ, NX, NC = 4, 8, 4, 2
T = 128
CAP = 40
W = 640
FF = 1024
SH = FF // (NX * NC)
ORDER = (0, 1, 2, -3, 4, 3, -2, -1)
PART = {off: u for u, off in enumerate(ORDER)}
YOFF = (0, 1, -1, 2)
YINV = (0, 2, 1, 3)
NU = len(ORDER)
ROWS = NY * CAP
HALF = ROWS // 2
PAD = 48
DEPTH = 6


def dot(a, b):
    return jnp.dot(a, b, preferred_element_type=F32)


def dot_nt(a, b):
    return lax.dot_general(a, b, (((1,), (1,)), ((), ())), preferred_element_type=F32)


def dot_tn(a, b):
    return lax.dot_general(a, b, (((0,), (0,)), ((), ())), preferred_element_type=F32)


def kernel(
    tok_hbm, cot_hbm, ids_hbm, vals_hbm, wg_hbm, wu_hbm, wd_hbm,
    tg_ref, gg, ug, dg,
    wg, wu, wd, ids, vals, infob, zx, zd, pt, grow,
    ys, xsr, xr, sr, hp, cr, t1, t2, gb, rs, rr, zs, zr, own, xt,
    info_s, zx_s, zd_s, zr_s, ys_s, rs_s, xa_s, xb_s,
    info_r, zx_r, zd_r, zr_r, ys_r, rs_r, c1_r, t1_r, t2_r, ag_r, af_r, cg_r, in_sem,
):
    tok = lax.axis_index("tok")
    exp = lax.axis_index("exp")
    y, z = tok // NZ, lax.rem(tok, NZ)
    x, core = exp // NC, lax.rem(exp, NC)

    def at_z(off):
        return (y * NZ + lax.rem(z + off + NZ, NZ), exp)

    def at_y(off):
        return (lax.rem(y + off + NY, NY) * NZ + z, exp)

    def col(off):
        return lax.rem(x + off + NX, NX)

    def at_x(off):
        return (tok, col(off) * NC + core)

    sibling = (tok, x * NC + (1 - core))

    def rc(src, dst, s, r, dev):
        return pltpu.make_async_remote_copy(
            src_ref=src, dst_ref=dst, send_sem=s, recv_sem=r, device_id=dev, device_id_type=MESH
        )

    def bytes_of(ref, sem):
        pltpu.make_async_copy(ref, ref, sem).wait()

    def ring_copy(buf, ss, rs_, off):
        step = 1 if off > 0 else -1
        k = off % NZ
        return rc(buf.at[(off - step) % NZ], buf.at[k], ss.at[0], rs_.at[k], at_z(-step))

    def info_copy(off):
        return ring_copy(infob, info_s, info_r, off)

    def zx_copy(off):
        return ring_copy(zx, zx_s, zx_r, off)

    def zd_copy(off):
        return ring_copy(zd, zd_s, zd_r, off)

    def zr_copy(off):
        k = off % NZ - 1
        return rc(zs.at[k], zr.at[k], zr_s.at[0], zr_r.at[k], at_z(1 if off == 4 else off))

    def ys_copy(u, k):
        return rc(ys.at[u, k - 1], xsr.at[u, YINV[k]], ys_s.at[u], ys_r.at[u], at_y(YOFF[k]))

    def rs_copy(u, k):
        return rc(rs.at[u, k - 1], rr.at[u, YINV[k]], rs_s.at[u], rs_r.at[u], at_y(YOFF[k]))

    def c1_copy(u):
        return rc(hp.at[u, 1 - core], cr.at[u], xa_s.at[u], c1_r.at[u], sibling)

    def x1_copy(u, n):
        src, dst, r, to = (
            (hp.at[u, core, col(2), 0], t1.at[u, 0], t1_r, 1),
            (hp.at[u, core, col(2), 1], t1.at[u, 1], t1_r, -1),
            (hp.at[u, core, col(1), 1], t2.at[u, 0, 1], t2_r, 1),
            (hp.at[u, core, col(-1), 0], t2.at[u, 1, 0], t2_r, -1),
            (hp.at[u, core, col(1), 0], t2.at[u, 0, 0], t2_r, 1),
            (hp.at[u, core, col(-1), 1], t2.at[u, 1, 1], t2_r, -1),
        )[n]
        return rc(src, dst, xb_s.at[u], r.at[u], at_x(to))

    def ag_send(u, n):
        part, r, to = (
            (gb.at[u, core, x], ag_r.at[u, 0], 1),
            (gb.at[u, core, x], ag_r.at[u, 1], -1),
            (gb.at[u, core, col(-1), 0], af_r.at[u], 1),
            (gb.at[u, core, col(1), 1], af_r.at[u], -1),
        )[n]
        return rc(part, part, xb_s.at[u], r, at_x(to))

    def cg_send(u, off):
        part = gb.at[u, core, col(off)]
        return rc(part, part, xa_s.at[u], cg_r.at[u], sibling)

    inputs = [
        pltpu.make_async_copy(src, dst, in_sem.at[n])
        for n, (src, dst) in enumerate(
            (
                (ids_hbm, ids),
                (vals_hbm, vals),
                (tok_hbm, zx.at[0]),
                (cot_hbm, zd.at[0]),
                (wg_hbm, wg),
                (wu_hbm, wu),
                (wd_hbm, wd),
            )
        )
    ]

    def make_tables(u):
        before = (
            lax.broadcasted_iota(jnp.int32, (T, T), 0) < lax.broadcasted_iota(jnp.int32, (T, T), 1)
        ).astype(BF16)
        block = infob[ORDER[u] % NZ]
        named, value = block[0:8], block[8:16]
        masks, gates = [], []
        for k in range(NY):
            expert = (lax.rem(y + YOFF[k] + NY, NY) * NZ + z).astype(F32)
            hit = named == expert
            masks.append(jnp.sum(jnp.where(hit, 1.0, 0.0), axis=0, keepdims=True))
            gates.append(jnp.sum(jnp.where(hit, value, 0.0), axis=0, keepdims=True))
        mask_all = jnp.concatenate(masks + [jnp.zeros((8 - NY, T), F32)], axis=0)
        rank_all = dot(mask_all.astype(BF16), before)
        want = lax.broadcasted_iota(jnp.int32, (CAP, T), 0).astype(F32)
        tables, gcols = [], []
        for k in range(NY):
            on = (rank_all[k : k + 1] == want) & (mask_all[k : k + 1] > 0.5)
            tables.append(jnp.where(on, 1.0, 0.0))
            gcols.append(jnp.sum(jnp.where(on, gates[k], 0.0), axis=1, keepdims=True))
        pt[u] = jnp.concatenate(tables, axis=0).astype(BF16)
        grow[u] = jnp.concatenate(gcols, axis=0)

    def enter():
        barrier = pltpu.get_barrier_semaphore()
        partners = [at_z(off) for off in (1, -1, 2, -2, 3, -3)]
        partners += [at_y(off) for off in (1, -1, 2)] + [at_x(1), at_x(-1), sibling]
        for dev in partners:
            pl.semaphore_signal(barrier, inc=1, device_id=dev, device_id_type=MESH)
        for copy in inputs:
            copy.start()
        for copy in inputs[:4]:
            copy.wait()
        nought = jnp.zeros((2, T), F32)
        infob[0] = jnp.concatenate([ids[...].astype(F32), nought - 1.0, vals[...], nought], axis=0)
        make_tables(0)
        gather(0)
        pl.semaphore_wait(barrier, len(partners))

    def gather(u):
        k = ORDER[u] % NZ
        xs = dot(pt[u], zx[k])
        ss = dot(pt[u], zd[k]) * grow[u]
        for k in range(NY):
            both = jnp.concatenate([xs[k * CAP : (k + 1) * CAP], ss[k * CAP : (k + 1) * CAP]], axis=0)
            if k == 0:
                xsr[u, 0] = both.astype(BF16)
            else:
                ys[u, k - 1] = both.astype(BF16)

    def send_rows(u):
        for k in (3, 1, 2):
            ys_copy(u, k).start()

    def place(u):
        make_tables(u)
        gather(u)
        send_rows(u)

    def pass_x(d):
        for off in (d, -d):
            info_copy(off).wait_recv()
            zx_copy(off).wait_recv()
            if d < 3 or off > 0:
                after = off + (1 if off > 0 else -1)
                info_copy(after).start()
                zx_copy(after).start()

    def pass_d(d):
        for off in (d, -d):
            zd_copy(off).wait_recv()
            if d < 3 or off < 0:
                zd_copy(off + (1 if off > 0 else -1)).start()

    def partial(u, a, value):
        value = value.astype(BF16)
        for s in range(NX * NC):
            hp[u, s % NC, s // NC, :, a] = value[:, s * SH : (s + 1) * SH].reshape(2, HALF, SH)

    def s0(u):
        bytes_of(xsr.at[u, 1:NY], ys_r.at[u])
        both = [xsr[u, j].astype(F32) for j in range(NY)]
        rows = jnp.concatenate([v[:CAP] for v in both], axis=0).astype(BF16)
        scaled = jnp.concatenate([v[CAP:] for v in both], axis=0).astype(BF16)
        xr[u] = rows
        sr[u] = scaled
        partial(u, 0, dot(rows, wg[...]))
        partial(u, 1, dot(rows, wu[...]))
        partial(u, 2, dot_nt(scaled, wd[...]))
        c1_copy(u).start()

    def s1(u):
        c1_copy(u).wait_recv()
        for off in (2, 1, -1, 0):
            xx = col(off)
            hp[u, core, xx] = (hp[u, core, xx].astype(F32) + cr[u, xx].astype(F32)).astype(BF16)
            for n in {2: (0, 1), 1: (2,), -1: (3,), 0: ()}[off]:
                x1_copy(u, n).start()

    def s2(u):
        bytes_of(t1.at[u], t1_r.at[u])
        for n, (off, half) in enumerate(((1, 0), (-1, 1))):
            xx = col(off)
            hp[u, core, xx, half] = (hp[u, core, xx, half].astype(F32) + t1[u, n].astype(F32)).astype(BF16)
            x1_copy(u, 4 + n).start()

    def s3(u):
        bytes_of(t2.at[u], t2_r.at[u])
        for half in range(2):
            h = hp[u, core, x, half].astype(F32) + t2[u, 0, half].astype(F32) + t2[u, 1, half].astype(F32)
            h_gate, h_up, d_act = h[0], h[1], h[2]
            sigma = 1.0 / (1.0 + jnp.exp(-h_gate))
            gb[u, core, x, half, 0] = (h_gate * sigma * h_up).astype(BF16)
            gb[u, core, x, half, 1] = (d_act * h_up * sigma * (1.0 + h_gate * (1.0 - sigma))).astype(BF16)
            gb[u, core, x, half, 2] = (d_act * h_gate * sigma).astype(BF16)
        ag_send(u, 0).start()
        ag_send(u, 1).start()
        cg_send(u, 0).start()

    def s4(u):
        bytes_of(gb.at[u, core, col(-1)], ag_r.at[u, 0])
        ag_send(u, 2).start()
        bytes_of(gb.at[u, core, col(1)], ag_r.at[u, 1])
        ag_send(u, 3).start()
        cg_send(u, -1).start()
        cg_send(u, 1).start()

    def s5(u):
        bytes_of(gb.at[u, core, col(2)], af_r.at[u])
        cg_send(u, 2).start()

    def hidden(u, a):
        return jnp.concatenate(
            [gb[u, s % NC, s // NC, :, a].reshape(ROWS, SH) for s in range(NX * NC)], axis=1
        )

    def s6(u):
        bytes_of(gb.at[u, 1 - core], cg_r.at[u])
        value = dot_nt(hidden(u, 1), wg[...]) + dot_nt(hidden(u, 2), wu[...])
        nought = jnp.zeros((PAD - CAP, W), F32)
        for k in (3, 1, 2, 0):
            slot = jnp.concatenate([value[k * CAP : (k + 1) * CAP], nought], axis=0).astype(BF16)
            if k == 0:
                rr[u, 0] = slot
            else:
                rs[u, k - 1] = slot
                rs_copy(u, k).start()

    def sent_u(u):
        bytes_of(hp.at[u], xa_s.at[u])
        bytes_of(hp.at[u, :, 0:3], xb_s.at[u])
        bytes_of(ys.at[u], ys_s.at[u])

    def sent_z():
        bytes_of(infob.at[0 : NZ - 1], info_s.at[0])
        bytes_of(zx.at[0 : NZ - 1], zx_s.at[0])
        bytes_of(zd.at[0 : NZ - 1], zd_s.at[0])

    def s7(u):
        bytes_of(rr.at[u, 1:NY], rs_r.at[u])
        rows = jnp.concatenate([rr[u, j].astype(F32)[:CAP] for j in range(NY)], axis=0).astype(BF16)
        value = dot_tn(pt[u], rows)
        if ORDER[u] == 0:
            own[...] = value
        else:
            zs[ORDER[u] % NZ - 1] = value.astype(BF16)
            if ORDER[u] != 3:
                zr_copy(ORDER[u]).start()

    def join():
        zr_copy(4).wait_recv()
        zs[2] = (zs[2].astype(F32) + zr[3].astype(F32)).astype(BF16)
        zr_copy(3).start()

    def step(s, carry):
        for k, stage, first in ((1, s1, 2), (5, s5, 0), (4, s4, 1), (3, s3, 1), (2, s2, 1)):

            @pl.when((s >= k + first) & (s < NU + k))
            def _(k=k, stage=stage):
                stage(s - k)

        @pl.when(s < NU)
        def _():
            s0(s)

        @pl.when((s >= DEPTH) & (s < NU + DEPTH))
        def _():
            s6(s - DEPTH)
            sent_u(s - DEPTH)

        for u in range(NU - 1):

            @pl.when(s == u + DEPTH + 1)
            def _(u=u):
                s7(u)

        for u in range(5, NU):

            @pl.when(s == u - 2)
            def _(u=u):
                place(u)

        @pl.when(s == NU)
        def _():
            sent_z()

        return carry

    enter()
    for off in (1, -1):
        info_copy(off).start()
    for off in (1, -1):
        zx_copy(off).start()
    send_rows(0)
    for off in (1, -1):
        zd_copy(off).start()
    for copy in inputs[4:]:
        copy.wait()
    s0(0)
    pass_x(1)
    pass_d(1)
    place(1)
    s1(0)
    pass_x(2)
    s2(0)
    pass_d(2)
    place(2)
    s3(0)
    s0(1)
    pass_x(3)
    s1(1)
    s4(0)
    pass_d(3)
    place(3)
    s0(2)
    info_copy(4).wait_recv()
    zx_copy(4).wait_recv()
    zd_copy(-4).wait_recv()
    place(4)
    lax.fori_loop(3, NU + DEPTH, step, 0)

    everything = xr[...].reshape(NU * ROWS, W)
    for n in range(W // 128):
        xt[n * 128 : (n + 1) * 128] = everything[:, n * 128 : (n + 1) * 128].T

    def all_rows(xx, a):
        return jnp.concatenate(
            [gb[:, cc, xx, :, a].reshape(NU * ROWS, SH) for cc in range(NC)], axis=1
        )

    def gate_step(xx, carry):
        at = pl.ds(pl.multiple_of(xx * 2 * SH, 2 * SH), 2 * SH)
        gg[:, at] = dot(xt[...], all_rows(xx, 1)).astype(BF16)
        return carry

    join()
    lax.fori_loop(0, NX, gate_step, 0)
    s7(NU - 1)

    def rest_step(xx, carry):
        at = pl.ds(pl.multiple_of(xx * 2 * SH, 2 * SH), 2 * SH)
        ug[:, at] = dot(xt[...], all_rows(xx, 2)).astype(BF16)
        dg[at, :] = dot_tn(all_rows(xx, 0), sr[...].reshape(NU * ROWS, W)).astype(BF16)
        return carry

    lax.fori_loop(0, NX, rest_step, 0)

    def finish():
        total = own[...]
        for off in (1, 2, -3, 3, -2, -1):
            zr_copy(off).wait_recv()
            total = total + zr[off % NZ - 1].astype(F32)
        tg_ref[...] = total.astype(BF16)
        bytes_of(zs, zr_s.at[0])
        for u in range(NU):
            bytes_of(rs.at[u], rs_s.at[u])

    finish()


def write_out(*refs):
    srcs, dsts, done = refs[:4], refs[4:8], refs[8]
    copies = [pltpu.make_async_copy(srcs[n], dsts[n], done.at[n]) for n in range(4)]
    for copy in copies:
        copy.start()
    for copy in copies:
        copy.wait()


def on_device(tokens, cotangent, routes, gate_values, w_gate, w_up, w_down):
    sem = pltpu.SemaphoreType.DMA

    def vm(*shape, dtype=BF16):
        return pltpu.VMEM(shape, dtype)

    vmem = pl.BlockSpec(memory_space=pltpu.VMEM)
    hbm = pl.BlockSpec(memory_space=pl.ANY)
    scratch = [
        vm(W, FF), vm(W, FF), vm(FF, W),
        vm(6, T, dtype=jnp.int32), vm(6, T, dtype=F32), vm(NZ, 16, T, dtype=F32),
        vm(NZ, T, W), vm(NZ, T, W),
        vm(NU, ROWS, T), vm(NU, ROWS, 1, dtype=F32),
        vm(NU, 3, 2 * CAP, W), vm(NU, NY, 2 * CAP, W),
        vm(NU, ROWS, W), vm(NU, ROWS, W),
        vm(NU, NC, NX, 2, 3, HALF, SH), vm(NU, NX, 2, 3, HALF, SH),
        vm(NU, 2, 3, HALF, SH), vm(NU, 2, 2, 3, HALF, SH),
        vm(NU, NC, NX, 2, 3, HALF, SH),
        vm(NU, 3, PAD, W), vm(NU, NY, PAD, W),
        vm(NZ - 1, T, W), vm(NZ - 1, T, W), vm(T, W, dtype=F32),
        vm(W, NU * ROWS),
    ]
    sems = [sem((1,)) for _ in range(4)]
    sems += [sem((NU,)) for _ in range(4)]
    sems += [sem((NZ,)), sem((NZ,)), sem((NZ,)), sem((NZ - 1,))]
    sems += [sem((NU,)) for _ in range(5)]
    sems += [sem((NU, 2)), sem((NU,)), sem((NU,)), sem((7,))]
    flops = 2 * NU * ROWS * W * FF * 8
    shapes = ((T, W), (W, FF), (W, FF), (FF, W))
    results = pl.pallas_call(
        kernel,
        out_shape=tuple(pltpu.VMEM(shape, BF16) for shape in shapes),
        in_specs=[pl.BlockSpec(memory_space=pltpu.HBM)] * 7,
        out_specs=(vmem, vmem, vmem, vmem),
        scratch_shapes=scratch + sems,
        compiler_params=pltpu.CompilerParams(
            collective_id=0, has_side_effects=True, vmem_limit_bytes=50 * 1024 * 1024
        ),
        cost_estimate=pl.CostEstimate(flops=flops, bytes_accessed=12_000_000, transcendentals=0),
    )(tokens, cotangent, routes.T, gate_values.T, w_gate[0], w_up[0], w_down[0])
    token_grad, gate_grad, up_grad, down_grad = pl.pallas_call(
        write_out,
        out_shape=tuple(jax.ShapeDtypeStruct(shape, BF16) for shape in shapes),
        in_specs=[hbm] * 4,
        out_specs=(hbm,) * 4,
        scratch_shapes=[sem((4,))],
        compiler_params=pltpu.CompilerParams(vmem_limit_bytes=1024 * 1024),
    )(*(pltpu.with_memory_space_constraint(r, pltpu.VMEM) for r in results))
    return (token_grad, gate_grad[None], up_grad[None], down_grad[None])


def solution(mesh):
    return jax.shard_map(
        on_device,
        mesh=mesh,
        in_specs=(
            P("tok", "exp"),
            P("tok", "exp"),
            P("tok", None),
            P("tok", None),
            P("tok", "exp", None),
            P("tok", "exp", None),
            P("tok", None, "exp"),
        ),
        out_specs=(
            P("tok", "exp"),
            P("tok", "exp", None),
            P("tok", "exp", None),
            P("tok", None, "exp"),
        ),
        check_vma=False,
    )
```

time: 303 us -> 122 us (0.40)
  waiting for transfers between devices: 198 us -> 0 us
  Pallas kernels: 0 us -> 117 us
  matrix products: 37.1 us -> 0 us
  starting transfers between devices: 35.5 us -> 0 us
  between operations: 14.3 us -> 0.65 us
  other arithmetic: 10.2 us -> 0 us
  local copies, waits for them, and re-layouts: 6 us -> 1.37 us
    pallas_call x0 -> x2, Pallas kernels: none -> 117 us  [the longest x1 115 us: on_device(): pl.pallas_call(kernel, out_shape=tuple((pltpu.VMEM(shape, BF16) for shape...]
    psum x1 -> x0, waiting for transfers between devices: 103 us -> none  [on_device(): lax.psum(part_up.astype(jnp.bfloat16), 'exp').astype(jnp.float32)]
    all_to_all x4 -> x0, waiting for transfers between devices: 94 us -> none  [the longest x1 35.8 us: on_device(): lax.all_to_all(x_send, 'tok', split_axis=0, concat_axis=0, tiled=True)]
    dot_general x11 -> x0, matrix products: 37.1 us -> none  [the longest x5 16 us: contract_rows(): lax.dot_general(left, right, (((0,), (0,)), ((), ())), preferred_element_...]
    all_to_all x4 -> x0, starting transfers between devices: 35.3 us -> none  [the longest x1 11.5 us: on_device(): lax.all_to_all(slot_gates.astype(jnp.bfloat16), 'tok', split_axis=0, conc...]
    convert_element_type x6 -> x0, other arithmetic: 5.67 us -> none  [the longest x1 4.91 us: hidden_math(): d_up = (d_act * h_gate * sigmoid_gate).astype(jnp.bfloat16)]
    unnamed x29 -> x4, local copies, waits for them, and re-layouts: 4.5 us -> 1.37 us
  transfers between devices with their start and end apart: 5 -> 0, of which waited for: 5 -> 0; matrix products, arithmetic and copies ran while one was open for 9% -> 0% of each run, Pallas kernels for 0% -> 0%
where the time goes in v2:
time: 122 us; the launch traced here: 119 us
  Pallas kernels  117 us (96%)
  local copies, waits for them, and re-layouts  1.37 us (1%)
    pallas_call x1, Pallas kernels, on_device(): pl.pallas_call(kernel, out_shape=tuple((pltpu.VMEM(shape, BF16) for shape...  115 us

profile of v2, /device:TPU:24, one launch (start us, length us, event | category | flops | bytes accessed | tf_op | source)
XLA Modules:
  0.0 119.3 jit_solution(12551733897079211828)
XLA Ops:
  0.6 0.0 copy-start
  0.6 0.7 copy-done
  1.3 0.0 copy-start.1
  1.3 0.7 copy-done.1
  2.0 115.3 %shard_map.102 = (bf16[128,640]{1,0:T(8,128)(2,1)S(1)}, bf16[640,1024]{1,0:T(8,128)(2,1)S(1)}, bf16[640,1024]{1,0:T(8,128)(2,1)S(1)}, bf16[1024,640]{1,0:T(8,128)(2,1)S(1)}) custom-call(bf16[128,640]{1,0:T(8,128)(2,1)} %tok_hbm.1, bf16[128,640]{1,0:T(8,128)(2,1)} %cot_hbm.1, s32[6,128]{1,0:T(8,128)S(1)} %bitcast.8, f32[6,128]{1,0:T(8,128)S(1)} %bitcast.9, ...), custom_call_target="tpu_custom_call" | custom-call | flops 13421772800 | bytes 12000000 | tf_op jit(solution)/shard_map/pallas_call | solution.py:459
  117.3 2.0 %shard_map.103 = (bf16[128,640]{1,0:T(8,128)(2,1)}, bf16[640,1024]{1,0:T(8,128)(2,1)}, bf16[640,1024]{1,0:T(8,128)(2,1)}, bf16[1024,640]{1,0:T(8,128)(2,1)}) custom-call(bf16[128,640]{1,0:T(8,128)(2,1)S(1)} %get-tuple-element.12.refs_0_, bf16[640,1024]{1,0:T(8,128)(2,1)S(1)} %get-tuple-element.13.refs_1_, bf16[640,1024]{1,0:T(8,128)(2,1)S(1)} %get-tuple-element.14.refs_2_, ...), custom_call_target="tpu_custom_call" | custom-call | tf_op jit(solution)/shard_map/pallas_call | solution.py:470
Async XLA Ops:
  0.6 0.7 copy-start
  1.3 0.7 copy-start.1

commit v3 on v2

--- a/solution.py
+++ b/solution.py
@@ -313,24 +313,30 @@
         zr_copy(3).start()
 
     def step(s, carry):
-        for k, stage, first in ((1, s1, 2), (5, s5, 0), (4, s4, 1), (3, s3, 1), (2, s2, 1)):
-
-            @pl.when((s >= k + first) & (s < NU + k))
-            def _(k=k, stage=stage):
-                stage(s - k)
-
-        @pl.when(s < NU)
+        def each(stage, lag, first=0):
+            @pl.when((s >= lag + first) & (s < NU + lag))
+            def _():
+                stage(s - lag)
+
+        each(s1, 1)
+        each(s5, 4)
+        each(s4, 3, 1)
+        each(s3, 2, 1)
+
+        @pl.when(s == 3)
         def _():
-            s0(s)
-
-        @pl.when((s >= DEPTH) & (s < NU + DEPTH))
-        def _():
-            s6(s - DEPTH)
-            sent_u(s - DEPTH)
-
-        for u in range(NU - 1):
-
-            @pl.when(s == u + DEPTH + 1)
+            info_copy(4).wait_recv()
+            zx_copy(4).wait_recv()
+            zd_copy(-4).wait_recv()
+            place(4)
+
+        each(s0, 0)
+        each(s2, 1)
+        each(s6, 4)
+        each(sent_u, 5)
+        for u in range(4):
+
+            @pl.when(s == u + 5)
             def _(u=u):
                 s7(u)
 
@@ -340,18 +346,14 @@
             def _(u=u):
                 place(u)
 
-        @pl.when(s == NU)
-        def _():
-            sent_z()
-
         return carry
 
     enter()
+    send_rows(0)
     for off in (1, -1):
         info_copy(off).start()
     for off in (1, -1):
         zx_copy(off).start()
-    send_rows(0)
     for off in (1, -1):
         zd_copy(off).start()
     for copy in inputs[4:]:
@@ -361,23 +363,36 @@
     pass_d(1)
     place(1)
     s1(0)
+    s2(0)
     pass_x(2)
-    s2(0)
     pass_d(2)
-    place(2)
     s3(0)
     s0(1)
-    pass_x(3)
+    place(2)
     s1(1)
     s4(0)
+    s2(1)
+    pass_x(3)
     pass_d(3)
     place(3)
     s0(2)
-    info_copy(4).wait_recv()
-    zx_copy(4).wait_recv()
-    zd_copy(-4).wait_recv()
-    place(4)
-    lax.fori_loop(3, NU + DEPTH, step, 0)
+    lax.fori_loop(3, NU + 1, step, 0)
+    s5(5)
+    s4(6)
+    s3(7)
+    s6(5)
+    s7(4)
+    s5(6)
+    s4(7)
+    s6(6)
+    s7(5)
+    s5(7)
+    s6(7)
+    sent_z()
+    for u in range(4, NU):
+        sent_u(u)
+    join()
+    s7(6)
 
     everything = xr[...].reshape(NU * ROWS, W)
     for n in range(W // 128):
@@ -393,17 +408,22 @@
         gg[:, at] = dot(xt[...], all_rows(xx, 1)).astype(BF16)
         return carry
 
-    join()
     lax.fori_loop(0, NX, gate_step, 0)
-    s7(NU - 1)
-
-    def rest_step(xx, carry):
+    s7(7)
+
+    def up_step(xx, carry):
         at = pl.ds(pl.multiple_of(xx * 2 * SH, 2 * SH), 2 * SH)
         ug[:, at] = dot(xt[...], all_rows(xx, 2)).astype(BF16)
+        return carry
+
+    lax.fori_loop(0, NX, up_step, 0)
+
+    def down_step(xx, carry):
+        at = pl.ds(pl.multiple_of(xx * 2 * SH, 2 * SH), 2 * SH)
         dg[at, :] = dot_tn(all_rows(xx, 0), sr[...].reshape(NU * ROWS, W)).astype(BF16)
         return carry
 
-    lax.fori_loop(0, NX, rest_step, 0)
+    lax.fori_loop(0, NX, down_step, 0)
 
     def finish():
         total = own[...]
@@ -420,11 +440,19 @@
 
 def write_out(*refs):
     srcs, dsts, done = refs[:4], refs[4:8], refs[8]
-    copies = [pltpu.make_async_copy(srcs[n], dsts[n], done.at[n]) for n in range(4)]
+    copies = []
+    for src, dst in zip(srcs, dsts):
+        for rows in range(0, src.shape[0], T):
+            part = pl.ds(rows, T)
+            copies.append(pltpu.make_async_copy(src.at[part], dst.at[part], done.at[len(copies)]))
     for copy in copies:
         copy.start()
     for copy in copies:
         copy.wait()
+
+
+def hbm_of(array):
+    return pltpu.with_memory_space_constraint(array, pltpu.HBM)
 
 
 def on_device(tokens, cotangent, routes, gate_values, w_gate, w_up, w_down):
@@ -466,13 +494,13 @@
             collective_id=0, has_side_effects=True, vmem_limit_bytes=50 * 1024 * 1024
         ),
         cost_estimate=pl.CostEstimate(flops=flops, bytes_accessed=12_000_000, transcendentals=0),
-    )(tokens, cotangent, routes.T, gate_values.T, w_gate[0], w_up[0], w_down[0])
+    )(tokens, cotangent, hbm_of(routes.T), hbm_of(gate_values.T), w_gate[0], w_up[0], w_down[0])
     token_grad, gate_grad, up_grad, down_grad = pl.pallas_call(
         write_out,
         out_shape=tuple(jax.ShapeDtypeStruct(shape, BF16) for shape in shapes),
         in_specs=[hbm] * 4,
         out_specs=(hbm,) * 4,
-        scratch_shapes=[sem((4,))],
+        scratch_shapes=[sem((sum(rows // T for rows, _ in shapes),))],
         compiler_params=pltpu.CompilerParams(vmem_limit_bytes=1024 * 1024),
     )(*(pltpu.with_memory_space_constraint(r, pltpu.VMEM) for r in results))
     return (token_grad, gate_grad[None], up_grad[None], down_grad[None])

time: 122 us -> 114 us (0.934)
  Pallas kernels: 117 us -> 111 us
  local copies, waits for them, and re-layouts: 1.37 us -> 0 us
    pallas_call x1, Pallas kernels: 115 us -> 109 us  [on_device(): pl.pallas_call(kernel, out_shape=tuple((pltpu.VMEM(shape, BF16) for shape...]
    unnamed x4 -> x0, local copies, waits for them, and re-layouts: 1.37 us -> none
where the time goes in v3:
time: 114 us; the launch traced here: 112 us
  Pallas kernels  111 us (97%)
    pallas_call x1, Pallas kernels, on_device(): pl.pallas_call(kernel, out_shape=tuple((pltpu.VMEM(shape, BF16) for shape...  109 us

profile of v3, /device:TPU:24, one launch (start us, length us, event | category | flops | bytes accessed | tf_op | source)
XLA Modules:
  0.0 111.7 jit_solution(7215415737962844866)
XLA Ops:
  0.6 108.8 %shard_map.102 = (bf16[128,640]{1,0:T(8,128)(2,1)S(1)}, bf16[640,1024]{1,0:T(8,128)(2,1)S(1)}, bf16[640,1024]{1,0:T(8,128)(2,1)S(1)}, bf16[1024,640]{1,0:T(8,128)(2,1)S(1)}) custom-call(bf16[128,640]{1,0:T(8,128)(2,1)} %tok_hbm.1, bf16[128,640]{1,0:T(8,128)(2,1)} %cot_hbm.1, s32[6,128]{1,0:T(8,128)} %bitcast.14, f32[6,128]{1,0:T(8,128)} %bitcast.15, ...), custom_call_target="tpu_custom_call" | custom-call | flops 13421772800 | bytes 12000000 | tf_op jit(solution)/shard_map/pallas_call | solution.py:487
  109.4 2.1 %shard_map.103 = (bf16[128,640]{1,0:T(8,128)(2,1)}, bf16[640,1024]{1,0:T(8,128)(2,1)}, bf16[640,1024]{1,0:T(8,128)(2,1)}, bf16[1024,640]{1,0:T(8,128)(2,1)}) custom-call(bf16[128,640]{1,0:T(8,128)(2,1)S(1)} %get-tuple-element.12.refs_0_, bf16[640,1024]{1,0:T(8,128)(2,1)S(1)} %get-tuple-element.13.refs_1_, bf16[640,1024]{1,0:T(8,128)(2,1)S(1)} %get-tuple-element.14.refs_2_, ...), custom_call_target="tpu_custom_call" | custom-call | tf_op jit(solution)/shard_map/pallas_call | solution.py:498

commit v4 on v3

--- a/solution.py
+++ b/solution.py
@@ -14,7 +14,7 @@
 W = 640
 FF = 1024
 SH = FF // (NX * NC)
-ORDER = (0, 1, 2, -3, 4, 3, -2, -1)
+ORDER = (0, 1, 2, -2, -3, 4, 3, -1)
 PART = {off: u for u, off in enumerate(ORDER)}
 YOFF = (0, 1, -1, 2)
 YINV = (0, 2, 1, 3)
@@ -91,13 +91,13 @@
         return rc(zs.at[k], zr.at[k], zr_s.at[0], zr_r.at[k], at_z(1 if off == 4 else off))
 
     def ys_copy(u, k):
-        return rc(ys.at[u, k - 1], xsr.at[u, YINV[k]], ys_s.at[u], ys_r.at[u], at_y(YOFF[k]))
+        return rc(ys.at[u, k - 1], xsr.at[u, YINV[k]], ys_s.at[0], ys_r.at[u], at_y(YOFF[k]))
 
     def rs_copy(u, k):
-        return rc(rs.at[u, k - 1], rr.at[u, YINV[k]], rs_s.at[u], rs_r.at[u], at_y(YOFF[k]))
+        return rc(rs.at[u, k - 1], rr.at[u, YINV[k]], rs_s.at[0], rs_r.at[u], at_y(YOFF[k]))
 
     def c1_copy(u):
-        return rc(hp.at[u, 1 - core], cr.at[u], xa_s.at[u], c1_r.at[u], sibling)
+        return rc(hp.at[u, 1 - core], cr.at[u], xa_s.at[0], c1_r.at[u], sibling)
 
     def x1_copy(u, n):
         src, dst, r, to = (
@@ -108,7 +108,7 @@
             (hp.at[u, core, col(1), 0], t2.at[u, 0, 0], t2_r, 1),
             (hp.at[u, core, col(-1), 1], t2.at[u, 1, 1], t2_r, -1),
         )[n]
-        return rc(src, dst, xb_s.at[u], r.at[u], at_x(to))
+        return rc(src, dst, xb_s.at[0], r.at[u], at_x(to))
 
     def ag_send(u, n):
         part, r, to = (
@@ -117,11 +117,11 @@
             (gb.at[u, core, col(-1), 0], af_r.at[u], 1),
             (gb.at[u, core, col(1), 1], af_r.at[u], -1),
         )[n]
-        return rc(part, part, xb_s.at[u], r, at_x(to))
+        return rc(part, part, xb_s.at[0], r, at_x(to))
 
     def cg_send(u, off):
         part = gb.at[u, core, col(off)]
-        return rc(part, part, xa_s.at[u], cg_r.at[u], sibling)
+        return rc(part, part, xa_s.at[0], cg_r.at[u], sibling)
 
     inputs = [
         pltpu.make_async_copy(src, dst, in_sem.at[n])
@@ -286,11 +286,6 @@
                 rs[u, k - 1] = slot
                 rs_copy(u, k).start()
 
-    def sent_u(u):
-        bytes_of(hp.at[u], xa_s.at[u])
-        bytes_of(hp.at[u, :, 0:3], xb_s.at[u])
-        bytes_of(ys.at[u], ys_s.at[u])
-
     def sent_z():
         bytes_of(infob.at[0 : NZ - 1], info_s.at[0])
         bytes_of(zx.at[0 : NZ - 1], zx_s.at[0])
@@ -325,15 +320,11 @@
 
         @pl.when(s == 3)
         def _():
-            info_copy(4).wait_recv()
-            zx_copy(4).wait_recv()
-            zd_copy(-4).wait_recv()
             place(4)
 
         each(s0, 0)
         each(s2, 1)
         each(s6, 4)
-        each(sent_u, 5)
         for u in range(4):
 
             @pl.when(s == u + 5)
@@ -344,6 +335,10 @@
 
             @pl.when(s == u - 2)
             def _(u=u):
+                if ORDER[u] == 4:
+                    info_copy(4).wait_recv()
+                    zx_copy(4).wait_recv()
+                    zd_copy(-4).wait_recv()
                 place(u)
 
         return carry
@@ -366,15 +361,15 @@
     s2(0)
     pass_x(2)
     pass_d(2)
+    place(2)
     s3(0)
     s0(1)
-    place(2)
     s1(1)
     s4(0)
+    place(3)
     s2(1)
     pass_x(3)
     pass_d(3)
-    place(3)
     s0(2)
     lax.fori_loop(3, NU + 1, step, 0)
     s5(5)
@@ -389,10 +384,8 @@
     s5(7)
     s6(7)
     sent_z()
-    for u in range(4, NU):
-        sent_u(u)
+    s7(6)
     join()
-    s7(6)
 
     everything = xr[...].reshape(NU * ROWS, W)
     for n in range(W // 128):
@@ -432,8 +425,10 @@
             total = total + zr[off % NZ - 1].astype(F32)
         tg_ref[...] = total.astype(BF16)
         bytes_of(zs, zr_s.at[0])
-        for u in range(NU):
-            bytes_of(rs.at[u], rs_s.at[u])
+        bytes_of(hp, xa_s.at[0])
+        bytes_of(hp.at[:, :, 0:3], xb_s.at[0])
+        bytes_of(ys, ys_s.at[0])
+        bytes_of(rs, rs_s.at[0])
 
     finish()
 
@@ -477,8 +472,7 @@
         vm(NZ - 1, T, W), vm(NZ - 1, T, W), vm(T, W, dtype=F32),
         vm(W, NU * ROWS),
     ]
-    sems = [sem((1,)) for _ in range(4)]
-    sems += [sem((NU,)) for _ in range(4)]
+    sems = [sem((1,)) for _ in range(8)]
     sems += [sem((NZ,)), sem((NZ,)), sem((NZ,)), sem((NZ - 1,))]
     sems += [sem((NU,)) for _ in range(5)]
     sems += [sem((NU, 2)), sem((NU,)), sem((NU,)), sem((7,))]

time: 114 us -> 113 us (level); the launches traced: 112 us -> 113 us
  no operation moved by 1% of the time
where the time goes in v4:
time: 113 us
  Pallas kernels  112 us (99%)
    pallas_call x1, Pallas kernels, on_device(): pl.pallas_call(kernel, out_shape=tuple((pltpu.VMEM(shape, BF16) for shape...  110 us

profile of v4, /device:TPU:24, one launch (start us, length us, event | category | flops | bytes accessed | tf_op | source)
XLA Modules:
  0.0 112.6 jit_solution(15648892812492599378)
XLA Ops:
  0.6 109.7 %shard_map.102 = (bf16[128,640]{1,0:T(8,128)(2,1)S(1)}, bf16[640,1024]{1,0:T(8,128)(2,1)S(1)}, bf16[640,1024]{1,0:T(8,128)(2,1)S(1)}, bf16[1024,640]{1,0:T(8,128)(2,1)S(1)}) custom-call(bf16[128,640]{1,0:T(8,128)(2,1)} %tok_hbm.1, bf16[128,640]{1,0:T(8,128)(2,1)} %cot_hbm.1, s32[6,128]{1,0:T(8,128)} %bitcast.14, f32[6,128]{1,0:T(8,128)} %bitcast.15, ...), custom_call_target="tpu_custom_call" | custom-call | flops 13421772800 | bytes 12000000 | tf_op jit(solution)/shard_map/pallas_call | solution.py:481
  110.3 2.1 %shard_map.103 = (bf16[128,640]{1,0:T(8,128)(2,1)}, bf16[640,1024]{1,0:T(8,128)(2,1)}, bf16[640,1024]{1,0:T(8,128)(2,1)}, bf16[1024,640]{1,0:T(8,128)(2,1)}) custom-call(bf16[128,640]{1,0:T(8,128)(2,1)S(1)} %get-tuple-element.12.refs_0_, bf16[640,1024]{1,0:T(8,128)(2,1)S(1)} %get-tuple-element.13.refs_1_, bf16[640,1024]{1,0:T(8,128)(2,1)S(1)} %get-tuple-element.14.refs_2_, ...), custom_call_target="tpu_custom_call" | custom-call | tf_op jit(solution)/shard_map/pallas_call | solution.py:492

commit v5 on v4

--- a/solution.py
+++ b/solution.py
@@ -401,8 +401,9 @@
         gg[:, at] = dot(xt[...], all_rows(xx, 1)).astype(BF16)
         return carry
 
-    lax.fori_loop(0, NX, gate_step, 0)
+    lax.fori_loop(0, NX // 2, gate_step, 0)
     s7(7)
+    lax.fori_loop(NX // 2, NX, gate_step, 0)
 
     def up_step(xx, carry):
         at = pl.ds(pl.multiple_of(xx * 2 * SH, 2 * SH), 2 * SH)

time: 113 us -> 113 us (level)
  no operation moved by 1% of the time
where the time goes in v5:
time: 113 us
  Pallas kernels  112 us (99%)
    pallas_call x1, Pallas kernels, on_device(): pl.pallas_call(kernel, out_shape=tuple((pltpu.VMEM(shape, BF16) for shape...  110 us

profile of v5, /device:TPU:24, one launch (start us, length us, event | category | flops | bytes accessed | tf_op | source)
XLA Modules:
  0.0 112.6 jit_solution(5424500334076923729)
XLA Ops:
  0.6 109.7 %shard_map.102 = (bf16[128,640]{1,0:T(8,128)(2,1)S(1)}, bf16[640,1024]{1,0:T(8,128)(2,1)S(1)}, bf16[640,1024]{1,0:T(8,128)(2,1)S(1)}, bf16[1024,640]{1,0:T(8,128)(2,1)S(1)}) custom-call(bf16[128,640]{1,0:T(8,128)(2,1)} %tok_hbm.1, bf16[128,640]{1,0:T(8,128)(2,1)} %cot_hbm.1, s32[6,128]{1,0:T(8,128)} %bitcast.14, f32[6,128]{1,0:T(8,128)} %bitcast.15, ...), custom_call_target="tpu_custom_call" | custom-call | flops 13421772800 | bytes 12000000 | tf_op jit(solution)/shard_map/pallas_call | solution.py:482
  110.3 2.1 %shard_map.103 = (bf16[128,640]{1,0:T(8,128)(2,1)}, bf16[640,1024]{1,0:T(8,128)(2,1)}, bf16[640,1024]{1,0:T(8,128)(2,1)}, bf16[1024,640]{1,0:T(8,128)(2,1)}) custom-call(bf16[128,640]{1,0:T(8,128)(2,1)S(1)} %get-tuple-element.12.refs_0_, bf16[640,1024]{1,0:T(8,128)(2,1)S(1)} %get-tuple-element.13.refs_1_, bf16[640,1024]{1,0:T(8,128)(2,1)S(1)} %get-tuple-element.14.refs_2_, ...), custom_call_target="tpu_custom_call" | custom-call | tf_op jit(solution)/shard_map/pallas_call | solution.py:493
